TPU v7x, 512 devices: a whole 4x8x8 slice. The times are simulated.
512 devices in a mesh: store: 32 (over z, y_lo, core), prod: 16 (over y_hi, x).
Axes of the slice: x: 4, y: 8 (y_hi: 4, y_lo: 2; y = y_hi * 2 + y_lo), z: 8, core: 2. Of those that a mesh axis runs over, the one named last changes fastest.
Arguments:
- gradients: bfloat16 [196608, 2048], P(('store', 'prod')), may hold values from -6 to 6
- destinations: int32 [196608], P(('store', 'prod')), may hold values from 0 to 31, as said below
- queries: bfloat16 [1536, 2048], P(('store', 'prod')), may hold values from -6 to 6
- left_factor: float32 [32, 32], replicated, may hold values from -11 to 11, as said below
- right_factor: float32 [64, 64], replicated, may hold values from -11 to 11, as said below
Outputs:
- scores: bfloat16 [1536, 393216], P(None, ('store', 'prod'))
Inputs may be any that keep to these rules, and one draw needn't show every extreme that they name: `destinations`: within the rows of one producer (aligned blocks of 384 rows) no store index is named more than 24 times, and one store index, the same for every producer, is named exactly 24 times in every block. `left_factor`: a dense real matrix. `right_factor`: a dense real matrix.
All inputs are finite; a program needn't handle non-finite values.
Results may differ from a plain program's by a relative error of at most 0.0049.
Values may be sent and summed in bfloat16 or wider, within the bound.
No kernel may reach another device: no remote copies, remote signals or barrier semaphores. Data moves between devices by JAX's collectives and lax.ppermute only.
A program may use at most 64 MiB of HBM per device.

v0:
```python
import math
import jax
import jax.numpy as jnp
from jax import lax
from jax.sharding import PartitionSpec as P


def from_behind(block, axis, distance):
    devices = range(lax.axis_size(axis))
    route = [((i - distance) % len(devices), i) for i in devices]
    return lax.ppermute(block, axis, route)


def precondition(gradients, left_factor, right_factor):
    left_size = left_factor.shape[0]
    right_size = right_factor.shape[0]
    leading = gradients.shape[:-1]
    matrices = gradients.astype(jnp.float32).reshape((-1, left_size, right_size))
    right_done = jnp.einsum("nbc,cd->nbd", matrices, right_factor, precision=lax.Precision.HIGHEST)
    product = jnp.einsum("ab,nbd->nad", left_factor, right_done, precision=lax.Precision.HIGHEST)
    product = product.reshape(leading + (left_size * right_size,))
    scaling = lax.rsqrt(jnp.mean(product * product, axis=-1, keepdims=True) + 1e-06)
    return (product * scaling * (1.0 / math.sqrt(left_size * right_size))).astype(jnp.bfloat16)


def row_ranks(targets, owners):
    matches = (targets[:, None] == jnp.arange(owners, dtype=jnp.int32)[None, :]).astype(jnp.int32)
    earlier = jnp.cumsum(matches, axis=0) - matches
    return jnp.sum(earlier * matches, axis=1)


def fill_tile(scores, local_block, position, stored):
    product = lax.dot_general(
        local_block, stored, (((1,), (1,)), ((), ())), preferred_element_type=jnp.float32
    )
    return lax.dynamic_update_slice_in_dim(
        scores, product.astype(jnp.bfloat16), position * local_block.shape[0], 0
    )


def body(gradients, destinations, queries, left_factor, right_factor):
    owners = lax.axis_size("store")
    own_index = lax.axis_index("store")
    row_count, feature_width = gradients.shape
    bucket = 2 * row_count // owners
    capacity = owners * bucket
    places = destinations * bucket + row_ranks(destinations, owners)
    local_queries = lax.all_gather(queries, "prod", axis=0, tiled=True)
    blank_scores = jnp.zeros((local_queries.shape[0] * owners, capacity), jnp.bfloat16)
    buffer = jnp.zeros((capacity, feature_width), jnp.bfloat16).at[places].set(gradients)
    buffer = buffer.reshape((owners, bucket, feature_width))
    stored = precondition(
        lax.all_to_all(buffer, "store", split_axis=0, concat_axis=0, tiled=True),
        left_factor,
        right_factor,
    ).reshape((capacity, feature_width))
    scores = fill_tile(blank_scores, local_queries, own_index, stored)

    def advance(turn_index, cycle_state):
        current, moving = cycle_state
        moving = from_behind(moving, "store", 1)
        current = fill_tile(current, moving, (own_index - turn_index) % owners, stored)
        return (current, moving)

    scores, moving = lax.fori_loop(1, owners, advance, (scores, local_queries))
    return scores


def solution(mesh):
    return jax.shard_map(
        body,
        mesh=mesh,
        in_specs=(
            P(("store", "prod"), None),
            P(("store", "prod")),
            P(("store", "prod"), None),
            P(),
            P(),
        ),
        out_specs=P(None, ("store", "prod")),
        check_vma=False,
    )
```

profile of v0, /device:TPU:258, one launch (start us, length us, event | category | flops | bytes accessed | tf_op | source)
XLA Modules:
  0.0 516.4 jit_solution(16796309453098849389)
XLA Ops:
  3.3 5.8 %scatter_custom_fusion = bf16[768,2048]{1,0:T(8,128)(2,1)} fusion(s32[384]{0:T(512)S(1)} %compare_select_fusion, bf16[384,2048]{1,0:T(8,128)(2,1)} %param.7, bf16[]{:T(256)} %constant.86.clone.1), kind=kCustom, calls=%fused_computation.12 | custom fusion | bytes 3146240 | tf_op jit(solution)/shard_map/scatter | solution.py:50
  9.2 8.5 %all-to-all-start = ((bf16[32,24,2048]{2,1,0:T(8,128)(2,1)}), bf16[32,24,2048]{2,1,0:T(8,128)(2,1)S(1)}, u32[]{:S(2)}, u32[]{:S(2)}) async-start(bf16[32,24,2048]{2,1,0:T(8,128)(2,1)} %bitcast.2), calls=%async_computation | async-start | bytes 6291456 | tf_op jit(solution)/shard_map/all_to_all | solution.py:53
  17.7 95.6 %all-gather = bf16[16,3,2048]{2,1,0:T(4,128)(2,1)S(1)} all-gather(bf16[1,3,2048]{2,1,0:T(4,128)(2,1)S(1)} %bitcast.52), channel_id=1, replica_groups=mesh['store'=32,'prod'=16] {'prod'}, dimensions={0}, use_global_device_ids=true | all-gather | bytes 208896 | tf_op jit(solution)/shard_map/all_gather | solution.py:48
  114.2 7.6 %reshape.42 = bf16[768,32,64]{2,1,0:T(8,128)(2,1)} reshape(bf16[32,24,2048]{2,1,0:T(8,128)(2,1)S(1)} %all-to-all-done) | data formatting | bytes 6291456 | tf_op jit(solution)/shard_map/reshape | solution.py:18
  121.9 9.0 %fusion.5 = f32[768,32,64]{0,2,1:T(8,128)S(1)} fusion(bf16[768,32,64]{2,1,0:T(8,128)(2,1)} %reshape.42, f32[64,64]{1,0:T(8,128)S(1)} %copy-done), kind=kOutput, calls=%fused_computation.8 | convolution fusion | flops 1207959552 | bytes 9453568 | tf_op jit(solution)/shard_map/nbc,cd->nbd/dot_general | solution.py:19
  130.9 10.1 %multiply_reduce_fusion = (f32[768]{0:T(1024)S(1)}, f32[768,32,64]{0,1,2:T(8,128)S(1)}) fusion(f32[32,32]{1,0:T(8,128)S(1)} %copy-done.2, f32[768,32,64]{0,2,1:T(8,128)S(1)} %fusion.5), kind=kOutput, calls=%fused_computation.10 | convolution fusion | flops 607124736 | bytes 12590080 | tf_op jit(solution)/shard_map/ab,nbd->nad/dot_general | solution.py:20
  141.0 3.9 copy.13
  144.9 2.4 fusion.2
  147.3 3.2 copy.14
  150.7 2.6 fusion.13
  154.7 361.7 %while.17 = (s32[]{:T(128)}, bf16[1536,768]{1,0:T(8,128)(2,1)}, bf16[48,2048]{1,0:T(8,128)(2,1)}, bf16[768,2048]{1,0:T(8,128)(2,1)S(1)}, s32[]{:T(128)}, /*index...) while((s32[]{:T(128)}, bf16[1536,768]{1,0:T(8,128)(2,1)}, ...), condition=%wide.region_6.7_spmd, body=%wide.region_5.6_spmd.sunk | while | flops 151031824 | bytes 4596032 | solution.py:65
  156.7 7.4 %collective-permute-done = bf16[48,2048]{1,0:T(8,128)(2,1)S(1)} collective-permute-done((bf16[48,2048]{1,0:T(8,128)(2,1)}, bf16[48,2048]{1,0:T(8,128)(2,1)S(1)}, u32[]{:S(2)}, u32[]{:S(2)}) %collective-permute-start) | collective-permute-done | bytes 196640 | tf_op jit(solution)/shard_map/while/body/eval_jaxpr/ppermute | solution.py:11
  166.4 1.9 collective-permute-start
  168.3 7.4 %collective-permute-done = bf16[48,2048]{1,0:T(8,128)(2,1)S(1)} collective-permute-done((bf16[48,2048]{1,0:T(8,128)(2,1)}, bf16[48,2048]{1,0:T(8,128)(2,1)S(1)}, u32[]{:S(2)}, u32[]{:S(2)}) %collective-permute-start) | collective-permute-done | bytes 196640 | tf_op jit(solution)/shard_map/while/body/eval_jaxpr/ppermute | solution.py:11
  180.0 7.4 %collective-permute-done = bf16[48,2048]{1,0:T(8,128)(2,1)S(1)} collective-permute-done((bf16[48,2048]{1,0:T(8,128)(2,1)}, bf16[48,2048]{1,0:T(8,128)(2,1)S(1)}, u32[]{:S(2)}, u32[]{:S(2)}) %collective-permute-start) | collective-permute-done | bytes 196640 | tf_op jit(solution)/shard_map/while/body/eval_jaxpr/ppermute | solution.py:11
  191.7 7.4 %collective-permute-done = bf16[48,2048]{1,0:T(8,128)(2,1)S(1)} collective-permute-done((bf16[48,2048]{1,0:T(8,128)(2,1)}, bf16[48,2048]{1,0:T(8,128)(2,1)S(1)}, u32[]{:S(2)}, u32[]{:S(2)}) %collective-permute-start) | collective-permute-done | bytes 196640 | tf_op jit(solution)/shard_map/while/body/eval_jaxpr/ppermute | solution.py:11
  203.3 7.4 %collective-permute-done = bf16[48,2048]{1,0:T(8,128)(2,1)S(1)} collective-permute-done((bf16[48,2048]{1,0:T(8,128)(2,1)}, bf16[48,2048]{1,0:T(8,128)(2,1)S(1)}, u32[]{:S(2)}, u32[]{:S(2)}) %collective-permute-start) | collective-permute-done | bytes 196640 | tf_op jit(solution)/shard_map/while/body/eval_jaxpr/ppermute | solution.py:11
  215.0 7.4 %collective-permute-done = bf16[48,2048]{1,0:T(8,128)(2,1)S(1)} collective-permute-done((bf16[48,2048]{1,0:T(8,128)(2,1)}, bf16[48,2048]{1,0:T(8,128)(2,1)S(1)}, u32[]{:S(2)}, u32[]{:S(2)}) %collective-permute-start) | collective-permute-done | bytes 196640 | tf_op jit(solution)/shard_map/while/body/eval_jaxpr/ppermute | solution.py:11
  224.7 1.9 collective-permute-start
  226.7 7.4 %collective-permute-done = bf16[48,2048]{1,0:T(8,128)(2,1)S(1)} collective-permute-done((bf16[48,2048]{1,0:T(8,128)(2,1)}, bf16[48,2048]{1,0:T(8,128)(2,1)S(1)}, u32[]{:S(2)}, u32[]{:S(2)}) %collective-permute-start) | collective-permute-done | bytes 196640 | tf_op jit(solution)/shard_map/while/body/eval_jaxpr/ppermute | solution.py:11
  236.4 1.9 collective-permute-start
  238.3 7.4 %collective-permute-done = bf16[48,2048]{1,0:T(8,128)(2,1)S(1)} collective-permute-done((bf16[48,2048]{1,0:T(8,128)(2,1)}, bf16[48,2048]{1,0:T(8,128)(2,1)S(1)}, u32[]{:S(2)}, u32[]{:S(2)}) %collective-permute-start) | collective-permute-done | bytes 196640 | tf_op jit(solution)/shard_map/while/body/eval_jaxpr/ppermute | solution.py:11
  248.1 1.9 collective-permute-start
  250.0 7.4 %collective-permute-done = bf16[48,2048]{1,0:T(8,128)(2,1)S(1)} collective-permute-done((bf16[48,2048]{1,0:T(8,128)(2,1)}, bf16[48,2048]{1,0:T(8,128)(2,1)S(1)}, u32[]{:S(2)}, u32[]{:S(2)}) %collective-permute-start) | collective-permute-done | bytes 196640 | tf_op jit(solution)/shard_map/while/body/eval_jaxpr/ppermute | solution.py:11
  259.7 1.9 collective-permute-start
  261.7 7.4 %collective-permute-done = bf16[48,2048]{1,0:T(8,128)(2,1)S(1)} collective-permute-done((bf16[48,2048]{1,0:T(8,128)(2,1)}, bf16[48,2048]{1,0:T(8,128)(2,1)S(1)}, u32[]{:S(2)}, u32[]{:S(2)}) %collective-permute-start) | collective-permute-done | bytes 196640 | tf_op jit(solution)/shard_map/while/body/eval_jaxpr/ppermute | solution.py:11
  271.4 1.9 collective-permute-start
  273.3 7.4 %collective-permute-done = bf16[48,2048]{1,0:T(8,128)(2,1)S(1)} collective-permute-done((bf16[48,2048]{1,0:T(8,128)(2,1)}, bf16[48,2048]{1,0:T(8,128)(2,1)S(1)}, u32[]{:S(2)}, u32[]{:S(2)}) %collective-permute-start) | collective-permute-done | bytes 196640 | tf_op jit(solution)/shard_map/while/body/eval_jaxpr/ppermute | solution.py:11
  285.0 7.4 %collective-permute-done = bf16[48,2048]{1,0:T(8,128)(2,1)S(1)} collective-permute-done((bf16[48,2048]{1,0:T(8,128)(2,1)}, bf16[48,2048]{1,0:T(8,128)(2,1)S(1)}, u32[]{:S(2)}, u32[]{:S(2)}) %collective-permute-start) | collective-permute-done | bytes 196640 | tf_op jit(solution)/shard_map/while/body/eval_jaxpr/ppermute | solution.py:11
  296.7 7.4 %collective-permute-done = bf16[48,2048]{1,0:T(8,128)(2,1)S(1)} collective-permute-done((bf16[48,2048]{1,0:T(8,128)(2,1)}, bf16[48,2048]{1,0:T(8,128)(2,1)S(1)}, u32[]{:S(2)}, u32[]{:S(2)}) %collective-permute-start) | collective-permute-done | bytes 196640 | tf_op jit(solution)/shard_map/while/body/eval_jaxpr/ppermute | solution.py:11
  308.3 7.4 %collective-permute-done = bf16[48,2048]{1,0:T(8,128)(2,1)S(1)} collective-permute-done((bf16[48,2048]{1,0:T(8,128)(2,1)}, bf16[48,2048]{1,0:T(8,128)(2,1)S(1)}, u32[]{:S(2)}, u32[]{:S(2)}) %collective-permute-start) | collective-permute-done | bytes 196640 | tf_op jit(solution)/shard_map/while/body/eval_jaxpr/ppermute | solution.py:11
  320.0 7.4 %collective-permute-done = bf16[48,2048]{1,0:T(8,128)(2,1)S(1)} collective-permute-done((bf16[48,2048]{1,0:T(8,128)(2,1)}, bf16[48,2048]{1,0:T(8,128)(2,1)S(1)}, u32[]{:S(2)}, u32[]{:S(2)}) %collective-permute-start) | collective-permute-done | bytes 196640 | tf_op jit(solution)/shard_map/while/body/eval_jaxpr/ppermute | solution.py:11
  331.7 7.4 %collective-permute-done = bf16[48,2048]{1,0:T(8,128)(2,1)S(1)} collective-permute-done((bf16[48,2048]{1,0:T(8,128)(2,1)}, bf16[48,2048]{1,0:T(8,128)(2,1)S(1)}, u32[]{:S(2)}, u32[]{:S(2)}) %collective-permute-start) | collective-permute-done | bytes 196640 | tf_op jit(solution)/shard_map/while/body/eval_jaxpr/ppermute | solution.py:11
  343.3 7.4 %collective-permute-done = bf16[48,2048]{1,0:T(8,128)(2,1)S(1)} collective-permute-done((bf16[48,2048]{1,0:T(8,128)(2,1)}, bf16[48,2048]{1,0:T(8,128)(2,1)S(1)}, u32[]{:S(2)}, u32[]{:S(2)}) %collective-permute-start) | collective-permute-done | bytes 196640 | tf_op jit(solution)/shard_map/while/body/eval_jaxpr/ppermute | solution.py:11
  355.0 7.4 %collective-permute-done = bf16[48,2048]{1,0:T(8,128)(2,1)S(1)} collective-permute-done((bf16[48,2048]{1,0:T(8,128)(2,1)}, bf16[48,2048]{1,0:T(8,128)(2,1)S(1)}, u32[]{:S(2)}, u32[]{:S(2)}) %collective-permute-start) | collective-permute-done | bytes 196640 | tf_op jit(solution)/shard_map/while/body/eval_jaxpr/ppermute | solution.py:11
  366.7 7.4 %collective-permute-done = bf16[48,2048]{1,0:T(8,128)(2,1)S(1)} collective-permute-done((bf16[48,2048]{1,0:T(8,128)(2,1)}, bf16[48,2048]{1,0:T(8,128)(2,1)S(1)}, u32[]{:S(2)}, u32[]{:S(2)}) %collective-permute-start) | collective-permute-done | bytes 196640 | tf_op jit(solution)/shard_map/while/body/eval_jaxpr/ppermute | solution.py:11
  378.3 7.4 %collective-permute-done = bf16[48,2048]{1,0:T(8,128)(2,1)S(1)} collective-permute-done((bf16[48,2048]{1,0:T(8,128)(2,1)}, bf16[48,2048]{1,0:T(8,128)(2,1)S(1)}, u32[]{:S(2)}, u32[]{:S(2)}) %collective-permute-start) | collective-permute-done | bytes 196640 | tf_op jit(solution)/shard_map/while/body/eval_jaxpr/ppermute | solution.py:11
  390.0 7.4 %collective-permute-done = bf16[48,2048]{1,0:T(8,128)(2,1)S(1)} collective-permute-done((bf16[48,2048]{1,0:T(8,128)(2,1)}, bf16[48,2048]{1,0:T(8,128)(2,1)S(1)}, u32[]{:S(2)}, u32[]{:S(2)}) %collective-permute-start) | collective-permute-done | bytes 196640 | tf_op jit(solution)/shard_map/while/body/eval_jaxpr/ppermute | solution.py:11
  401.7 7.4 %collective-permute-done = bf16[48,2048]{1,0:T(8,128)(2,1)S(1)} collective-permute-done((bf16[48,2048]{1,0:T(8,128)(2,1)}, bf16[48,2048]{1,0:T(8,128)(2,1)S(1)}, u32[]{:S(2)}, u32[]{:S(2)}) %collective-permute-start) | collective-permute-done | bytes 196640 | tf_op jit(solution)/shard_map/while/body/eval_jaxpr/ppermute | solution.py:11
  413.3 7.4 %collective-permute-done = bf16[48,2048]{1,0:T(8,128)(2,1)S(1)} collective-permute-done((bf16[48,2048]{1,0:T(8,128)(2,1)}, bf16[48,2048]{1,0:T(8,128)(2,1)S(1)}, u32[]{:S(2)}, u32[]{:S(2)}) %collective-permute-start) | collective-permute-done | bytes 196640 | tf_op jit(solution)/shard_map/while/body/eval_jaxpr/ppermute | solution.py:11
  425.0 7.4 %collective-permute-done = bf16[48,2048]{1,0:T(8,128)(2,1)S(1)} collective-permute-done((bf16[48,2048]{1,0:T(8,128)(2,1)}, bf16[48,2048]{1,0:T(8,128)(2,1)S(1)}, u32[]{:S(2)}, u32[]{:S(2)}) %collective-permute-start) | collective-permute-done | bytes 196640 | tf_op jit(solution)/shard_map/while/body/eval_jaxpr/ppermute | solution.py:11
  436.7 7.4 %collective-permute-done = bf16[48,2048]{1,0:T(8,128)(2,1)S(1)} collective-permute-done((bf16[48,2048]{1,0:T(8,128)(2,1)}, bf16[48,2048]{1,0:T(8,128)(2,1)S(1)}, u32[]{:S(2)}, u32[]{:S(2)}) %collective-permute-start) | collective-permute-done | bytes 196640 | tf_op jit(solution)/shard_map/while/body/eval_jaxpr/ppermute | solution.py:11
  448.3 7.4 %collective-permute-done = bf16[48,2048]{1,0:T(8,128)(2,1)S(1)} collective-permute-done((bf16[48,2048]{1,0:T(8,128)(2,1)}, bf16[48,2048]{1,0:T(8,128)(2,1)S(1)}, u32[]{:S(2)}, u32[]{:S(2)}) %collective-permute-start) | collective-permute-done | bytes 196640 | tf_op jit(solution)/shard_map/while/body/eval_jaxpr/ppermute | solution.py:11
  460.0 7.4 %collective-permute-done = bf16[48,2048]{1,0:T(8,128)(2,1)S(1)} collective-permute-done((bf16[48,2048]{1,0:T(8,128)(2,1)}, bf16[48,2048]{1,0:T(8,128)(2,1)S(1)}, u32[]{:S(2)}, u32[]{:S(2)}) %collective-permute-start) | collective-permute-done | bytes 196640 | tf_op jit(solution)/shard_map/while/body/eval_jaxpr/ppermute | solution.py:11
  471.7 7.4 %collective-permute-done = bf16[48,2048]{1,0:T(8,128)(2,1)S(1)} collective-permute-done((bf16[48,2048]{1,0:T(8,128)(2,1)}, bf16[48,2048]{1,0:T(8,128)(2,1)S(1)}, u32[]{:S(2)}, u32[]{:S(2)}) %collective-permute-start) | collective-permute-done | bytes 196640 | tf_op jit(solution)/shard_map/while/body/eval_jaxpr/ppermute | solution.py:11
  483.3 7.4 %collective-permute-done = bf16[48,2048]{1,0:T(8,128)(2,1)S(1)} collective-permute-done((bf16[48,2048]{1,0:T(8,128)(2,1)}, bf16[48,2048]{1,0:T(8,128)(2,1)S(1)}, u32[]{:S(2)}, u32[]{:S(2)}) %collective-permute-start) | collective-permute-done | bytes 196640 | tf_op jit(solution)/shard_map/while/body/eval_jaxpr/ppermute | solution.py:11
  495.0 7.4 %collective-permute-done = bf16[48,2048]{1,0:T(8,128)(2,1)S(1)} collective-permute-done((bf16[48,2048]{1,0:T(8,128)(2,1)}, bf16[48,2048]{1,0:T(8,128)(2,1)S(1)}, u32[]{:S(2)}, u32[]{:S(2)}) %collective-permute-start) | collective-permute-done | bytes 196640 | tf_op jit(solution)/shard_map/while/body/eval_jaxpr/ppermute | solution.py:11
  506.7 7.4 %collective-permute-done = bf16[48,2048]{1,0:T(8,128)(2,1)S(1)} collective-permute-done((bf16[48,2048]{1,0:T(8,128)(2,1)}, bf16[48,2048]{1,0:T(8,128)(2,1)S(1)}, u32[]{:S(2)}, u32[]{:S(2)}) %collective-permute-start) | collective-permute-done | bytes 196640 | tf_op jit(solution)/shard_map/while/body/eval_jaxpr/ppermute | solution.py:11
  (105 shorter events, 126.8 us)
Async XLA Ops:
  0.0 121.9 %copy-start = (f32[64,64]{1,0:T(8,128)S(1)}, f32[64,64]{1,0:T(8,128)}, u32[]{:S(2)}) copy-start(f32[64,64]{1,0:T(8,128)} %param.11) | copy-start | bytes 49156
  9.1 8.6 %copy-start.3 = (bf16[3,2048]{1,0:T(4,128)(2,1)S(1)}, bf16[3,2048]{1,0:T(4,128)(2,1)}, u32[]{:S(2)}) copy-start(bf16[3,2048]{1,0:T(4,128)(2,1)} %param.9) | copy-start | bytes 36868
  9.2 105.1 %all-to-all-start = ((bf16[32,24,2048]{2,1,0:T(8,128)(2,1)}), bf16[32,24,2048]{2,1,0:T(8,128)(2,1)S(1)}, u32[]{:S(2)}, u32[]{:S(2)}) async-start(bf16[32,24,2048]{2,1,0:T(8,128)(2,1)} %bitcast.2), calls=%async_computation | async-start | bytes 6291456 | tf_op jit(solution)/shard_map/all_to_all | solution.py:53
  121.9 9.0 %copy-start.2 = (f32[32,32]{1,0:T(8,128)S(1)}, f32[32,32]{1,0:T(8,128)}, u32[]{:S(2)}) copy-start(f32[32,32]{1,0:T(8,128)} %param.10) | copy-start | bytes 12292
  153.3 1.4 copy-start.1
  154.7 9.3 %collective-permute-start = (bf16[48,2048]{1,0:T(8,128)(2,1)}, bf16[48,2048]{1,0:T(8,128)(2,1)S(1)}, u32[]{:S(2)}, u32[]{:S(2)}) collective-permute-start(bf16[48,2048]{1,0:T(8,128)(2,1)} %get-tuple-element.205), channel_id=1, source_target_pairs={{496,0},{0,16},{16,32},{32,48},{48,64},{64,80},{80,96},{96,112},{1... | collective-permute-start | bytes 589832 | tf_op jit(solution)/shard_map/while/body/eval_jaxpr/ppermute | solution.py:11
  166.4 9.3 %collective-permute-start = (bf16[48,2048]{1,0:T(8,128)(2,1)}, bf16[48,2048]{1,0:T(8,128)(2,1)S(1)}, u32[]{:S(2)}, u32[]{:S(2)}) collective-permute-start(bf16[48,2048]{1,0:T(8,128)(2,1)} %get-tuple-element.205), channel_id=1, source_target_pairs={{496,0},{0,16},{16,32},{32,48},{48,64},{64,80},{80,96},{96,112},{1... | collective-permute-start | bytes 589832 | tf_op jit(solution)/shard_map/while/body/eval_jaxpr/ppermute | solution.py:11
  178.1 9.3 %collective-permute-start = (bf16[48,2048]{1,0:T(8,128)(2,1)}, bf16[48,2048]{1,0:T(8,128)(2,1)S(1)}, u32[]{:S(2)}, u32[]{:S(2)}) collective-permute-start(bf16[48,2048]{1,0:T(8,128)(2,1)} %get-tuple-element.205), channel_id=1, source_target_pairs={{496,0},{0,16},{16,32},{32,48},{48,64},{64,80},{80,96},{96,112},{1... | collective-permute-start | bytes 589832 | tf_op jit(solution)/shard_map/while/body/eval_jaxpr/ppermute | solution.py:11
  189.7 9.3 %collective-permute-start = (bf16[48,2048]{1,0:T(8,128)(2,1)}, bf16[48,2048]{1,0:T(8,128)(2,1)S(1)}, u32[]{:S(2)}, u32[]{:S(2)}) collective-permute-start(bf16[48,2048]{1,0:T(8,128)(2,1)} %get-tuple-element.205), channel_id=1, source_target_pairs={{496,0},{0,16},{16,32},{32,48},{48,64},{64,80},{80,96},{96,112},{1... | collective-permute-start | bytes 589832 | tf_op jit(solution)/shard_map/while/body/eval_jaxpr/ppermute | solution.py:11
  201.4 9.3 %collective-permute-start = (bf16[48,2048]{1,0:T(8,128)(2,1)}, bf16[48,2048]{1,0:T(8,128)(2,1)S(1)}, u32[]{:S(2)}, u32[]{:S(2)}) collective-permute-start(bf16[48,2048]{1,0:T(8,128)(2,1)} %get-tuple-element.205), channel_id=1, source_target_pairs={{496,0},{0,16},{16,32},{32,48},{48,64},{64,80},{80,96},{96,112},{1... | collective-permute-start | bytes 589832 | tf_op jit(solution)/shard_map/while/body/eval_jaxpr/ppermute | solution.py:11
  213.1 9.3 %collective-permute-start = (bf16[48,2048]{1,0:T(8,128)(2,1)}, bf16[48,2048]{1,0:T(8,128)(2,1)S(1)}, u32[]{:S(2)}, u32[]{:S(2)}) collective-permute-start(bf16[48,2048]{1,0:T(8,128)(2,1)} %get-tuple-element.205), channel_id=1, source_target_pairs={{496,0},{0,16},{16,32},{32,48},{48,64},{64,80},{80,96},{96,112},{1... | collective-permute-start | bytes 589832 | tf_op jit(solution)/shard_map/while/body/eval_jaxpr/ppermute | solution.py:11
  224.7 9.3 %collective-permute-start = (bf16[48,2048]{1,0:T(8,128)(2,1)}, bf16[48,2048]{1,0:T(8,128)(2,1)S(1)}, u32[]{:S(2)}, u32[]{:S(2)}) collective-permute-start(bf16[48,2048]{1,0:T(8,128)(2,1)} %get-tuple-element.205), channel_id=1, source_target_pairs={{496,0},{0,16},{16,32},{32,48},{48,64},{64,80},{80,96},{96,112},{1... | collective-permute-start | bytes 589832 | tf_op jit(solution)/shard_map/while/body/eval_jaxpr/ppermute | solution.py:11
  236.4 9.3 %collective-permute-start = (bf16[48,2048]{1,0:T(8,128)(2,1)}, bf16[48,2048]{1,0:T(8,128)(2,1)S(1)}, u32[]{:S(2)}, u32[]{:S(2)}) collective-permute-start(bf16[48,2048]{1,0:T(8,128)(2,1)} %get-tuple-element.205), channel_id=1, source_target_pairs={{496,0},{0,16},{16,32},{32,48},{48,64},{64,80},{80,96},{96,112},{1... | collective-permute-start | bytes 589832 | tf_op jit(solution)/shard_map/while/body/eval_jaxpr/ppermute | solution.py:11
  248.1 9.3 %collective-permute-start = (bf16[48,2048]{1,0:T(8,128)(2,1)}, bf16[48,2048]{1,0:T(8,128)(2,1)S(1)}, u32[]{:S(2)}, u32[]{:S(2)}) collective-permute-start(bf16[48,2048]{1,0:T(8,128)(2,1)} %get-tuple-element.205), channel_id=1, source_target_pairs={{496,0},{0,16},{16,32},{32,48},{48,64},{64,80},{80,96},{96,112},{1... | collective-permute-start | bytes 589832 | tf_op jit(solution)/shard_map/while/body/eval_jaxpr/ppermute | solution.py:11
  259.7 9.3 %collective-permute-start = (bf16[48,2048]{1,0:T(8,128)(2,1)}, bf16[48,2048]{1,0:T(8,128)(2,1)S(1)}, u32[]{:S(2)}, u32[]{:S(2)}) collective-permute-start(bf16[48,2048]{1,0:T(8,128)(2,1)} %get-tuple-element.205), channel_id=1, source_target_pairs={{496,0},{0,16},{16,32},{32,48},{48,64},{64,80},{80,96},{96,112},{1... | collective-permute-start | bytes 589832 | tf_op jit(solution)/shard_map/while/body/eval_jaxpr/ppermute | solution.py:11
  271.4 9.3 %collective-permute-start = (bf16[48,2048]{1,0:T(8,128)(2,1)}, bf16[48,2048]{1,0:T(8,128)(2,1)S(1)}, u32[]{:S(2)}, u32[]{:S(2)}) collective-permute-start(bf16[48,2048]{1,0:T(8,128)(2,1)} %get-tuple-element.205), channel_id=1, source_target_pairs={{496,0},{0,16},{16,32},{32,48},{48,64},{64,80},{80,96},{96,112},{1... | collective-permute-start | bytes 589832 | tf_op jit(solution)/shard_map/while/body/eval_jaxpr/ppermute | solution.py:11
  283.1 9.3 %collective-permute-start = (bf16[48,2048]{1,0:T(8,128)(2,1)}, bf16[48,2048]{1,0:T(8,128)(2,1)S(1)}, u32[]{:S(2)}, u32[]{:S(2)}) collective-permute-start(bf16[48,2048]{1,0:T(8,128)(2,1)} %get-tuple-element.205), channel_id=1, source_target_pairs={{496,0},{0,16},{16,32},{32,48},{48,64},{64,80},{80,96},{96,112},{1... | collective-permute-start | bytes 589832 | tf_op jit(solution)/shard_map/while/body/eval_jaxpr/ppermute | solution.py:11
  294.7 9.3 %collective-permute-start = (bf16[48,2048]{1,0:T(8,128)(2,1)}, bf16[48,2048]{1,0:T(8,128)(2,1)S(1)}, u32[]{:S(2)}, u32[]{:S(2)}) collective-permute-start(bf16[48,2048]{1,0:T(8,128)(2,1)} %get-tuple-element.205), channel_id=1, source_target_pairs={{496,0},{0,16},{16,32},{32,48},{48,64},{64,80},{80,96},{96,112},{1... | collective-permute-start | bytes 589832 | tf_op jit(solution)/shard_map/while/body/eval_jaxpr/ppermute | solution.py:11
  306.4 9.3 %collective-permute-start = (bf16[48,2048]{1,0:T(8,128)(2,1)}, bf16[48,2048]{1,0:T(8,128)(2,1)S(1)}, u32[]{:S(2)}, u32[]{:S(2)}) collective-permute-start(bf16[48,2048]{1,0:T(8,128)(2,1)} %get-tuple-element.205), channel_id=1, source_target_pairs={{496,0},{0,16},{16,32},{32,48},{48,64},{64,80},{80,96},{96,112},{1... | collective-permute-start | bytes 589832 | tf_op jit(solution)/shard_map/while/body/eval_jaxpr/ppermute | solution.py:11
  318.1 9.3 %collective-permute-start = (bf16[48,2048]{1,0:T(8,128)(2,1)}, bf16[48,2048]{1,0:T(8,128)(2,1)S(1)}, u32[]{:S(2)}, u32[]{:S(2)}) collective-permute-start(bf16[48,2048]{1,0:T(8,128)(2,1)} %get-tuple-element.205), channel_id=1, source_target_pairs={{496,0},{0,16},{16,32},{32,48},{48,64},{64,80},{80,96},{96,112},{1... | collective-permute-start | bytes 589832 | tf_op jit(solution)/shard_map/while/body/eval_jaxpr/ppermute | solution.py:11
  329.7 9.3 %collective-permute-start = (bf16[48,2048]{1,0:T(8,128)(2,1)}, bf16[48,2048]{1,0:T(8,128)(2,1)S(1)}, u32[]{:S(2)}, u32[]{:S(2)}) collective-permute-start(bf16[48,2048]{1,0:T(8,128)(2,1)} %get-tuple-element.205), channel_id=1, source_target_pairs={{496,0},{0,16},{16,32},{32,48},{48,64},{64,80},{80,96},{96,112},{1... | collective-permute-start | bytes 589832 | tf_op jit(solution)/shard_map/while/body/eval_jaxpr/ppermute | solution.py:11
  341.4 9.3 %collective-permute-start = (bf16[48,2048]{1,0:T(8,128)(2,1)}, bf16[48,2048]{1,0:T(8,128)(2,1)S(1)}, u32[]{:S(2)}, u32[]{:S(2)}) collective-permute-start(bf16[48,2048]{1,0:T(8,128)(2,1)} %get-tuple-element.205), channel_id=1, source_target_pairs={{496,0},{0,16},{16,32},{32,48},{48,64},{64,80},{80,96},{96,112},{1... | collective-permute-start | bytes 589832 | tf_op jit(solution)/shard_map/while/body/eval_jaxpr/ppermute | solution.py:11
  353.1 9.3 %collective-permute-start = (bf16[48,2048]{1,0:T(8,128)(2,1)}, bf16[48,2048]{1,0:T(8,128)(2,1)S(1)}, u32[]{:S(2)}, u32[]{:S(2)}) collective-permute-start(bf16[48,2048]{1,0:T(8,128)(2,1)} %get-tuple-element.205), channel_id=1, source_target_pairs={{496,0},{0,16},{16,32},{32,48},{48,64},{64,80},{80,96},{96,112},{1... | collective-permute-start | bytes 589832 | tf_op jit(solution)/shard_map/while/body/eval_jaxpr/ppermute | solution.py:11
  364.7 9.3 %collective-permute-start = (bf16[48,2048]{1,0:T(8,128)(2,1)}, bf16[48,2048]{1,0:T(8,128)(2,1)S(1)}, u32[]{:S(2)}, u32[]{:S(2)}) collective-permute-start(bf16[48,2048]{1,0:T(8,128)(2,1)} %get-tuple-element.205), channel_id=1, source_target_pairs={{496,0},{0,16},{16,32},{32,48},{48,64},{64,80},{80,96},{96,112},{1... | collective-permute-start | bytes 589832 | tf_op jit(solution)/shard_map/while/body/eval_jaxpr/ppermute | solution.py:11
  376.4 9.3 %collective-permute-start = (bf16[48,2048]{1,0:T(8,128)(2,1)}, bf16[48,2048]{1,0:T(8,128)(2,1)S(1)}, u32[]{:S(2)}, u32[]{:S(2)}) collective-permute-start(bf16[48,2048]{1,0:T(8,128)(2,1)} %get-tuple-element.205), channel_id=1, source_target_pairs={{496,0},{0,16},{16,32},{32,48},{48,64},{64,80},{80,96},{96,112},{1... | collective-permute-start | bytes 589832 | tf_op jit(solution)/shard_map/while/body/eval_jaxpr/ppermute | solution.py:11
  388.1 9.3 %collective-permute-start = (bf16[48,2048]{1,0:T(8,128)(2,1)}, bf16[48,2048]{1,0:T(8,128)(2,1)S(1)}, u32[]{:S(2)}, u32[]{:S(2)}) collective-permute-start(bf16[48,2048]{1,0:T(8,128)(2,1)} %get-tuple-element.205), channel_id=1, source_target_pairs={{496,0},{0,16},{16,32},{32,48},{48,64},{64,80},{80,96},{96,112},{1... | collective-permute-start | bytes 589832 | tf_op jit(solution)/shard_map/while/body/eval_jaxpr/ppermute | solution.py:11
  399.7 9.3 %collective-permute-start = (bf16[48,2048]{1,0:T(8,128)(2,1)}, bf16[48,2048]{1,0:T(8,128)(2,1)S(1)}, u32[]{:S(2)}, u32[]{:S(2)}) collective-permute-start(bf16[48,2048]{1,0:T(8,128)(2,1)} %get-tuple-element.205), channel_id=1, source_target_pairs={{496,0},{0,16},{16,32},{32,48},{48,64},{64,80},{80,96},{96,112},{1... | collective-permute-start | bytes 589832 | tf_op jit(solution)/shard_map/while/body/eval_jaxpr/ppermute | solution.py:11
  411.4 9.3 %collective-permute-start = (bf16[48,2048]{1,0:T(8,128)(2,1)}, bf16[48,2048]{1,0:T(8,128)(2,1)S(1)}, u32[]{:S(2)}, u32[]{:S(2)}) collective-permute-start(bf16[48,2048]{1,0:T(8,128)(2,1)} %get-tuple-element.205), channel_id=1, source_target_pairs={{496,0},{0,16},{16,32},{32,48},{48,64},{64,80},{80,96},{96,112},{1... | collective-permute-start | bytes 589832 | tf_op jit(solution)/shard_map/while/body/eval_jaxpr/ppermute | solution.py:11
  423.1 9.3 %collective-permute-start = (bf16[48,2048]{1,0:T(8,128)(2,1)}, bf16[48,2048]{1,0:T(8,128)(2,1)S(1)}, u32[]{:S(2)}, u32[]{:S(2)}) collective-permute-start(bf16[48,2048]{1,0:T(8,128)(2,1)} %get-tuple-element.205), channel_id=1, source_target_pairs={{496,0},{0,16},{16,32},{32,48},{48,64},{64,80},{80,96},{96,112},{1... | collective-permute-start | bytes 589832 | tf_op jit(solution)/shard_map/while/body/eval_jaxpr/ppermute | solution.py:11
  434.7 9.3 %collective-permute-start = (bf16[48,2048]{1,0:T(8,128)(2,1)}, bf16[48,2048]{1,0:T(8,128)(2,1)S(1)}, u32[]{:S(2)}, u32[]{:S(2)}) collective-permute-start(bf16[48,2048]{1,0:T(8,128)(2,1)} %get-tuple-element.205), channel_id=1, source_target_pairs={{496,0},{0,16},{16,32},{32,48},{48,64},{64,80},{80,96},{96,112},{1... | collective-permute-start | bytes 589832 | tf_op jit(solution)/shard_map/while/body/eval_jaxpr/ppermute | solution.py:11
  446.4 9.3 %collective-permute-start = (bf16[48,2048]{1,0:T(8,128)(2,1)}, bf16[48,2048]{1,0:T(8,128)(2,1)S(1)}, u32[]{:S(2)}, u32[]{:S(2)}) collective-permute-start(bf16[48,2048]{1,0:T(8,128)(2,1)} %get-tuple-element.205), channel_id=1, source_target_pairs={{496,0},{0,16},{16,32},{32,48},{48,64},{64,80},{80,96},{96,112},{1... | collective-permute-start | bytes 589832 | tf_op jit(solution)/shard_map/while/body/eval_jaxpr/ppermute | solution.py:11
  458.1 9.3 %collective-permute-start = (bf16[48,2048]{1,0:T(8,128)(2,1)}, bf16[48,2048]{1,0:T(8,128)(2,1)S(1)}, u32[]{:S(2)}, u32[]{:S(2)}) collective-permute-start(bf16[48,2048]{1,0:T(8,128)(2,1)} %get-tuple-element.205), channel_id=1, source_target_pairs={{496,0},{0,16},{16,32},{32,48},{48,64},{64,80},{80,96},{96,112},{1... | collective-permute-start | bytes 589832 | tf_op jit(solution)/shard_map/while/body/eval_jaxpr/ppermute | solution.py:11
  469.7 9.3 %collective-permute-start = (bf16[48,2048]{1,0:T(8,128)(2,1)}, bf16[48,2048]{1,0:T(8,128)(2,1)S(1)}, u32[]{:S(2)}, u32[]{:S(2)}) collective-permute-start(bf16[48,2048]{1,0:T(8,128)(2,1)} %get-tuple-element.205), channel_id=1, source_target_pairs={{496,0},{0,16},{16,32},{32,48},{48,64},{64,80},{80,96},{96,112},{1... | collective-permute-start | bytes 589832 | tf_op jit(solution)/shard_map/while/body/eval_jaxpr/ppermute | solution.py:11
  481.4 9.3 %collective-permute-start = (bf16[48,2048]{1,0:T(8,128)(2,1)}, bf16[48,2048]{1,0:T(8,128)(2,1)S(1)}, u32[]{:S(2)}, u32[]{:S(2)}) collective-permute-start(bf16[48,2048]{1,0:T(8,128)(2,1)} %get-tuple-element.205), channel_id=1, source_target_pairs={{496,0},{0,16},{16,32},{32,48},{48,64},{64,80},{80,96},{96,112},{1... | collective-permute-start | bytes 589832 | tf_op jit(solution)/shard_map/while/body/eval_jaxpr/ppermute | solution.py:11
  493.1 9.3 %collective-permute-start = (bf16[48,2048]{1,0:T(8,128)(2,1)}, bf16[48,2048]{1,0:T(8,128)(2,1)S(1)}, u32[]{:S(2)}, u32[]{:S(2)}) collective-permute-start(bf16[48,2048]{1,0:T(8,128)(2,1)} %get-tuple-element.205), channel_id=1, source_target_pairs={{496,0},{0,16},{16,32},{32,48},{48,64},{64,80},{80,96},{96,112},{1... | collective-permute-start | bytes 589832 | tf_op jit(solution)/shard_map/while/body/eval_jaxpr/ppermute | solution.py:11
  504.7 9.3 %collective-permute-start = (bf16[48,2048]{1,0:T(8,128)(2,1)}, bf16[48,2048]{1,0:T(8,128)(2,1)S(1)}, u32[]{:S(2)}, u32[]{:S(2)}) collective-permute-start(bf16[48,2048]{1,0:T(8,128)(2,1)} %get-tuple-element.205), channel_id=1, source_target_pairs={{496,0},{0,16},{16,32},{32,48},{48,64},{64,80},{80,96},{96,112},{1... | collective-permute-start | bytes 589832 | tf_op jit(solution)/shard_map/while/body/eval_jaxpr/ppermute | solution.py:11
where the time goes:
time: 518 us; the launch traced here: 516 us
  waiting for transfers between devices  228 us (44%)
  blocking collectives  95.6 us (18%)
  matrix products  74.3 us (14%)
  starting transfers between devices  67.7 us (13%)
  local copies, waits for them, and re-layouts  44.1 us (9%)
  other arithmetic  5.48 us (1%)
    ppermute x31, waiting for transfers between devices, from_behind(): return lax.ppermute(block, axis, route)  228 us
    all_gather x1, blocking collectives, body(): local_queries = lax.all_gather(queries, 'prod', axis=0, tiled=True)  95.6 us
    ppermute x31, starting transfers between devices, from_behind(): return lax.ppermute(block, axis, route)  59.1 us
    dot_general x32, matrix products, fill_tile(): lax.dot_general(local_block, stored, (((1,), (1,)), ((), ())), preferred_...  55.2 us
    while x31, local copies, waits for them, and re-layouts  20.9 us
  transfers between devices with their start and end apart: 32, of which 31 were waited for; matrix products, arithmetic and copies ran while one was open for 0% of the time, Pallas kernels for 0%

commit v1 on v0

--- a/solution.py
+++ b/solution.py
@@ -45,7 +45,12 @@
     bucket = 2 * row_count // owners
     capacity = owners * bucket
     places = destinations * bucket + row_ranks(destinations, owners)
-    local_queries = lax.all_gather(queries, "prod", axis=0, tiled=True)
+    local_queries = jnp.concatenate(
+        lax.all_to_all(
+            jnp.stack([queries for _ in range(lax.axis_size("prod"))], axis=0), "prod", 0, 0
+        ),
+        0,
+    )
     blank_scores = jnp.zeros((local_queries.shape[0] * owners, capacity), jnp.bfloat16)
     buffer = jnp.zeros((capacity, feature_width), jnp.bfloat16).at[places].set(gradients)
     buffer = buffer.reshape((owners, bucket, feature_width))

time: 518 us -> 524 us (1.012)
  the two profiles are of different devices: /device:TPU:258 before, /device:TPU:16 now
where the time goes in v1:
time: 524 us; the launch traced here: 523 us
  waiting for transfers between devices  312 us (60%)
  starting transfers between devices  79.8 us (15%)
  matrix products  74.3 us (14%)
  local copies, waits for them, and re-layouts  49 us (9%)
  other arithmetic  6.44 us (1%)
    ppermute x31, waiting for transfers between devices, from_behind(): return lax.ppermute(block, axis, route)  228 us
    all_to_all x1, waiting for transfers between devices, body(): lax.all_to_all(buffer, 'store', split_axis=0, concat_axis=0, tiled=True)  82 us
    ppermute x31, starting transfers between devices, from_behind(): return lax.ppermute(block, axis, route)  59.1 us
    dot_general x32, matrix products, fill_tile(): lax.dot_general(local_block, stored, (((1,), (1,)), ((), ())), preferred_...  55.2 us
    while x31, local copies, waits for them, and re-layouts  20.9 us
    all_to_all x1, starting transfers between devices, body(): lax.all_to_all(buffer, 'store', split_axis=0, concat_axis=0, tiled=True)  10.7 us
  transfers between devices with their start and end apart: 33, of which 33 were waited for; matrix products, arithmetic and copies ran while one was open for 2% of the time, Pallas kernels for 0%

profile of v1, /device:TPU:16, one launch (start us, length us, event | category | flops | bytes accessed | tf_op | source)
XLA Modules:
  0.0 523.1 jit_solution(13592031051531053660)
XLA Ops:
  1.5 9.9 %all-to-all-start.1 = ((bf16[16,3,2048]{2,1,0:T(4,128)(2,1)}), bf16[16,3,2048]{2,1,0:T(4,128)(2,1)S(1)}, u32[]{:S(2)}, u32[]{:S(2)}) async-start(bf16[16,3,2048]{2,1,0:T(4,128)(2,1)} %stack.2), calls=%async_computation.1 | async-start | bytes 524288 | tf_op jit(solution)/shard_map/all_to_all | solution.py:49
  14.7 5.8 %scatter_custom_fusion = bf16[768,2048]{1,0:T(8,128)(2,1)} fusion(s32[384]{0:T(512)S(1)} %compare_select_fusion, bf16[384,2048]{1,0:T(8,128)(2,1)} %param.7, bf16[]{:T(256)} %constant.86.clone.1), kind=kCustom, calls=%fused_computation.13 | custom fusion | bytes 3146240 | tf_op jit(solution)/shard_map/scatter | solution.py:55
  20.6 2.3 all-to-all-done.1
  22.9 10.7 %all-to-all-start = ((bf16[32,24,2048]{2,1,0:T(8,128)(2,1)}), bf16[32,24,2048]{2,1,0:T(8,128)(2,1)S(1)}, u32[]{:S(2)}, u32[]{:S(2)}) async-start(bf16[32,24,2048]{2,1,0:T(8,128)(2,1)} %bitcast.2), calls=%async_computation | async-start | bytes 6291456 | tf_op jit(solution)/shard_map/all_to_all | solution.py:58
  34.5 82.0 %all-to-all-done = bf16[32,24,2048]{2,1,0:T(8,128)(2,1)S(1)} async-done(((bf16[32,24,2048]{2,1,0:T(8,128)(2,1)}), bf16[32,24,2048]{2,1,0:T(8,128)(2,1)S(1)}, u32[]{:S(2)}, u32[]{:S(2)}) %all-to-all-start) | async-done | bytes 3145760 | tf_op jit(solution)/shard_map/all_to_all | solution.py:58
  116.5 7.6 %reshape.53 = bf16[768,32,64]{2,1,0:T(8,128)(2,1)} reshape(bf16[32,24,2048]{2,1,0:T(8,128)(2,1)S(1)} %all-to-all-done) | data formatting | bytes 6291456 | tf_op jit(solution)/shard_map/reshape | solution.py:18
  124.1 9.0 %fusion.5 = f32[768,32,64]{0,2,1:T(8,128)S(1)} fusion(bf16[768,32,64]{2,1,0:T(8,128)(2,1)} %reshape.53, f32[64,64]{1,0:T(8,128)S(1)} %copy-done), kind=kOutput, calls=%fused_computation.8 | convolution fusion | flops 1207959552 | bytes 9453568 | tf_op jit(solution)/shard_map/nbc,cd->nbd/dot_general | solution.py:19
  133.2 10.1 %multiply_reduce_fusion = (f32[768]{0:T(1024)S(1)}, f32[768,32,64]{0,1,2:T(8,128)S(1)}) fusion(f32[32,32]{1,0:T(8,128)S(1)} %copy-done.2, f32[768,32,64]{0,2,1:T(8,128)S(1)} %fusion.5), kind=kOutput, calls=%fused_computation.11 | convolution fusion | flops 607124736 | bytes 12590080 | tf_op jit(solution)/shard_map/ab,nbd->nad/dot_general | solution.py:20
  143.3 3.9 copy.8
  148.1 3.4 copy.7
  151.6 2.4 fusion.2
  154.0 3.2 copy.9
  157.3 2.6 fusion.13
  161.4 361.7 %while.17 = (s32[]{:T(128)}, bf16[1536,768]{1,0:T(8,128)(2,1)}, bf16[48,2048]{1,0:T(8,128)(2,1)}, bf16[768,2048]{1,0:T(8,128)(2,1)S(1)}, s32[]{:T(128)}, /*index...) while((s32[]{:T(128)}, bf16[1536,768]{1,0:T(8,128)(2,1)}, ...), condition=%wide.region_6.7_spmd, body=%wide.region_5.6_spmd.sunk | while | flops 151031824 | bytes 4596032 | solution.py:70
  163.3 7.4 %collective-permute-done = bf16[48,2048]{1,0:T(8,128)(2,1)S(1)} collective-permute-done((bf16[48,2048]{1,0:T(8,128)(2,1)}, bf16[48,2048]{1,0:T(8,128)(2,1)S(1)}, u32[]{:S(2)}, u32[]{:S(2)}) %collective-permute-start) | collective-permute-done | bytes 196640 | tf_op jit(solution)/shard_map/while/body/eval_jaxpr/ppermute | solution.py:11
  173.1 1.9 collective-permute-start
  175.0 7.4 %collective-permute-done = bf16[48,2048]{1,0:T(8,128)(2,1)S(1)} collective-permute-done((bf16[48,2048]{1,0:T(8,128)(2,1)}, bf16[48,2048]{1,0:T(8,128)(2,1)S(1)}, u32[]{:S(2)}, u32[]{:S(2)}) %collective-permute-start) | collective-permute-done | bytes 196640 | tf_op jit(solution)/shard_map/while/body/eval_jaxpr/ppermute | solution.py:11
  184.7 1.9 collective-permute-start
  186.7 7.4 %collective-permute-done = bf16[48,2048]{1,0:T(8,128)(2,1)S(1)} collective-permute-done((bf16[48,2048]{1,0:T(8,128)(2,1)}, bf16[48,2048]{1,0:T(8,128)(2,1)S(1)}, u32[]{:S(2)}, u32[]{:S(2)}) %collective-permute-start) | collective-permute-done | bytes 196640 | tf_op jit(solution)/shard_map/while/body/eval_jaxpr/ppermute | solution.py:11
  196.4 1.9 collective-permute-start
  198.3 7.4 %collective-permute-done = bf16[48,2048]{1,0:T(8,128)(2,1)S(1)} collective-permute-done((bf16[48,2048]{1,0:T(8,128)(2,1)}, bf16[48,2048]{1,0:T(8,128)(2,1)S(1)}, u32[]{:S(2)}, u32[]{:S(2)}) %collective-permute-start) | collective-permute-done | bytes 196640 | tf_op jit(solution)/shard_map/while/body/eval_jaxpr/ppermute | solution.py:11
  210.0 7.4 %collective-permute-done = bf16[48,2048]{1,0:T(8,128)(2,1)S(1)} collective-permute-done((bf16[48,2048]{1,0:T(8,128)(2,1)}, bf16[48,2048]{1,0:T(8,128)(2,1)S(1)}, u32[]{:S(2)}, u32[]{:S(2)}) %collective-permute-start) | collective-permute-done | bytes 196640 | tf_op jit(solution)/shard_map/while/body/eval_jaxpr/ppermute | solution.py:11
  221.7 7.4 %collective-permute-done = bf16[48,2048]{1,0:T(8,128)(2,1)S(1)} collective-permute-done((bf16[48,2048]{1,0:T(8,128)(2,1)}, bf16[48,2048]{1,0:T(8,128)(2,1)S(1)}, u32[]{:S(2)}, u32[]{:S(2)}) %collective-permute-start) | collective-permute-done | bytes 196640 | tf_op jit(solution)/shard_map/while/body/eval_jaxpr/ppermute | solution.py:11
  233.3 7.4 %collective-permute-done = bf16[48,2048]{1,0:T(8,128)(2,1)S(1)} collective-permute-done((bf16[48,2048]{1,0:T(8,128)(2,1)}, bf16[48,2048]{1,0:T(8,128)(2,1)S(1)}, u32[]{:S(2)}, u32[]{:S(2)}) %collective-permute-start) | collective-permute-done | bytes 196640 | tf_op jit(solution)/shard_map/while/body/eval_jaxpr/ppermute | solution.py:11
  245.0 7.4 %collective-permute-done = bf16[48,2048]{1,0:T(8,128)(2,1)S(1)} collective-permute-done((bf16[48,2048]{1,0:T(8,128)(2,1)}, bf16[48,2048]{1,0:T(8,128)(2,1)S(1)}, u32[]{:S(2)}, u32[]{:S(2)}) %collective-permute-start) | collective-permute-done | bytes 196640 | tf_op jit(solution)/shard_map/while/body/eval_jaxpr/ppermute | solution.py:11
  256.7 7.4 %collective-permute-done = bf16[48,2048]{1,0:T(8,128)(2,1)S(1)} collective-permute-done((bf16[48,2048]{1,0:T(8,128)(2,1)}, bf16[48,2048]{1,0:T(8,128)(2,1)S(1)}, u32[]{:S(2)}, u32[]{:S(2)}) %collective-permute-start) | collective-permute-done | bytes 196640 | tf_op jit(solution)/shard_map/while/body/eval_jaxpr/ppermute | solution.py:11
  268.3 7.4 %collective-permute-done = bf16[48,2048]{1,0:T(8,128)(2,1)S(1)} collective-permute-done((bf16[48,2048]{1,0:T(8,128)(2,1)}, bf16[48,2048]{1,0:T(8,128)(2,1)S(1)}, u32[]{:S(2)}, u32[]{:S(2)}) %collective-permute-start) | collective-permute-done | bytes 196640 | tf_op jit(solution)/shard_map/while/body/eval_jaxpr/ppermute | solution.py:11
  280.0 7.4 %collective-permute-done = bf16[48,2048]{1,0:T(8,128)(2,1)S(1)} collective-permute-done((bf16[48,2048]{1,0:T(8,128)(2,1)}, bf16[48,2048]{1,0:T(8,128)(2,1)S(1)}, u32[]{:S(2)}, u32[]{:S(2)}) %collective-permute-start) | collective-permute-done | bytes 196640 | tf_op jit(solution)/shard_map/while/body/eval_jaxpr/ppermute | solution.py:11
  291.7 7.4 %collective-permute-done = bf16[48,2048]{1,0:T(8,128)(2,1)S(1)} collective-permute-done((bf16[48,2048]{1,0:T(8,128)(2,1)}, bf16[48,2048]{1,0:T(8,128)(2,1)S(1)}, u32[]{:S(2)}, u32[]{:S(2)}) %collective-permute-start) | collective-permute-done | bytes 196640 | tf_op jit(solution)/shard_map/while/body/eval_jaxpr/ppermute | solution.py:11
  303.3 7.4 %collective-permute-done = bf16[48,2048]{1,0:T(8,128)(2,1)S(1)} collective-permute-done((bf16[48,2048]{1,0:T(8,128)(2,1)}, bf16[48,2048]{1,0:T(8,128)(2,1)S(1)}, u32[]{:S(2)}, u32[]{:S(2)}) %collective-permute-start) | collective-permute-done | bytes 196640 | tf_op jit(solution)/shard_map/while/body/eval_jaxpr/ppermute | solution.py:11
  315.0 7.4 %collective-permute-done = bf16[48,2048]{1,0:T(8,128)(2,1)S(1)} collective-permute-done((bf16[48,2048]{1,0:T(8,128)(2,1)}, bf16[48,2048]{1,0:T(8,128)(2,1)S(1)}, u32[]{:S(2)}, u32[]{:S(2)}) %collective-permute-start) | collective-permute-done | bytes 196640 | tf_op jit(solution)/shard_map/while/body/eval_jaxpr/ppermute | solution.py:11
  326.7 7.4 %collective-permute-done = bf16[48,2048]{1,0:T(8,128)(2,1)S(1)} collective-permute-done((bf16[48,2048]{1,0:T(8,128)(2,1)}, bf16[48,2048]{1,0:T(8,128)(2,1)S(1)}, u32[]{:S(2)}, u32[]{:S(2)}) %collective-permute-start) | collective-permute-done | bytes 196640 | tf_op jit(solution)/shard_map/while/body/eval_jaxpr/ppermute | solution.py:11
  338.3 7.4 %collective-permute-done = bf16[48,2048]{1,0:T(8,128)(2,1)S(1)} collective-permute-done((bf16[48,2048]{1,0:T(8,128)(2,1)}, bf16[48,2048]{1,0:T(8,128)(2,1)S(1)}, u32[]{:S(2)}, u32[]{:S(2)}) %collective-permute-start) | collective-permute-done | bytes 196640 | tf_op jit(solution)/shard_map/while/body/eval_jaxpr/ppermute | solution.py:11
  350.0 7.4 %collective-permute-done = bf16[48,2048]{1,0:T(8,128)(2,1)S(1)} collective-permute-done((bf16[48,2048]{1,0:T(8,128)(2,1)}, bf16[48,2048]{1,0:T(8,128)(2,1)S(1)}, u32[]{:S(2)}, u32[]{:S(2)}) %collective-permute-start) | collective-permute-done | bytes 196640 | tf_op jit(solution)/shard_map/while/body/eval_jaxpr/ppermute | solution.py:11
  361.7 7.4 %collective-permute-done = bf16[48,2048]{1,0:T(8,128)(2,1)S(1)} collective-permute-done((bf16[48,2048]{1,0:T(8,128)(2,1)}, bf16[48,2048]{1,0:T(8,128)(2,1)S(1)}, u32[]{:S(2)}, u32[]{:S(2)}) %collective-permute-start) | collective-permute-done | bytes 196640 | tf_op jit(solution)/shard_map/while/body/eval_jaxpr/ppermute | solution.py:11
  373.3 7.4 %collective-permute-done = bf16[48,2048]{1,0:T(8,128)(2,1)S(1)} collective-permute-done((bf16[48,2048]{1,0:T(8,128)(2,1)}, bf16[48,2048]{1,0:T(8,128)(2,1)S(1)}, u32[]{:S(2)}, u32[]{:S(2)}) %collective-permute-start) | collective-permute-done | bytes 196640 | tf_op jit(solution)/shard_map/while/body/eval_jaxpr/ppermute | solution.py:11
  385.0 7.4 %collective-permute-done = bf16[48,2048]{1,0:T(8,128)(2,1)S(1)} collective-permute-done((bf16[48,2048]{1,0:T(8,128)(2,1)}, bf16[48,2048]{1,0:T(8,128)(2,1)S(1)}, u32[]{:S(2)}, u32[]{:S(2)}) %collective-permute-start) | collective-permute-done | bytes 196640 | tf_op jit(solution)/shard_map/while/body/eval_jaxpr/ppermute | solution.py:11
  396.7 7.4 %collective-permute-done = bf16[48,2048]{1,0:T(8,128)(2,1)S(1)} collective-permute-done((bf16[48,2048]{1,0:T(8,128)(2,1)}, bf16[48,2048]{1,0:T(8,128)(2,1)S(1)}, u32[]{:S(2)}, u32[]{:S(2)}) %collective-permute-start) | collective-permute-done | bytes 196640 | tf_op jit(solution)/shard_map/while/body/eval_jaxpr/ppermute | solution.py:11
  408.3 7.4 %collective-permute-done = bf16[48,2048]{1,0:T(8,128)(2,1)S(1)} collective-permute-done((bf16[48,2048]{1,0:T(8,128)(2,1)}, bf16[48,2048]{1,0:T(8,128)(2,1)S(1)}, u32[]{:S(2)}, u32[]{:S(2)}) %collective-permute-start) | collective-permute-done | bytes 196640 | tf_op jit(solution)/shard_map/while/body/eval_jaxpr/ppermute | solution.py:11
  420.0 7.4 %collective-permute-done = bf16[48,2048]{1,0:T(8,128)(2,1)S(1)} collective-permute-done((bf16[48,2048]{1,0:T(8,128)(2,1)}, bf16[48,2048]{1,0:T(8,128)(2,1)S(1)}, u32[]{:S(2)}, u32[]{:S(2)}) %collective-permute-start) | collective-permute-done | bytes 196640 | tf_op jit(solution)/shard_map/while/body/eval_jaxpr/ppermute | solution.py:11
  431.7 7.4 %collective-permute-done = bf16[48,2048]{1,0:T(8,128)(2,1)S(1)} collective-permute-done((bf16[48,2048]{1,0:T(8,128)(2,1)}, bf16[48,2048]{1,0:T(8,128)(2,1)S(1)}, u32[]{:S(2)}, u32[]{:S(2)}) %collective-permute-start) | collective-permute-done | bytes 196640 | tf_op jit(solution)/shard_map/while/body/eval_jaxpr/ppermute | solution.py:11
  443.3 7.4 %collective-permute-done = bf16[48,2048]{1,0:T(8,128)(2,1)S(1)} collective-permute-done((bf16[48,2048]{1,0:T(8,128)(2,1)}, bf16[48,2048]{1,0:T(8,128)(2,1)S(1)}, u32[]{:S(2)}, u32[]{:S(2)}) %collective-permute-start) | collective-permute-done | bytes 196640 | tf_op jit(solution)/shard_map/while/body/eval_jaxpr/ppermute | solution.py:11
  455.0 7.4 %collective-permute-done = bf16[48,2048]{1,0:T(8,128)(2,1)S(1)} collective-permute-done((bf16[48,2048]{1,0:T(8,128)(2,1)}, bf16[48,2048]{1,0:T(8,128)(2,1)S(1)}, u32[]{:S(2)}, u32[]{:S(2)}) %collective-permute-start) | collective-permute-done | bytes 196640 | tf_op jit(solution)/shard_map/while/body/eval_jaxpr/ppermute | solution.py:11
  466.7 7.4 %collective-permute-done = bf16[48,2048]{1,0:T(8,128)(2,1)S(1)} collective-permute-done((bf16[48,2048]{1,0:T(8,128)(2,1)}, bf16[48,2048]{1,0:T(8,128)(2,1)S(1)}, u32[]{:S(2)}, u32[]{:S(2)}) %collective-permute-start) | collective-permute-done | bytes 196640 | tf_op jit(solution)/shard_map/while/body/eval_jaxpr/ppermute | solution.py:11
  478.3 7.4 %collective-permute-done = bf16[48,2048]{1,0:T(8,128)(2,1)S(1)} collective-permute-done((bf16[48,2048]{1,0:T(8,128)(2,1)}, bf16[48,2048]{1,0:T(8,128)(2,1)S(1)}, u32[]{:S(2)}, u32[]{:S(2)}) %collective-permute-start) | collective-permute-done | bytes 196640 | tf_op jit(solution)/shard_map/while/body/eval_jaxpr/ppermute | solution.py:11
  490.0 7.4 %collective-permute-done = bf16[48,2048]{1,0:T(8,128)(2,1)S(1)} collective-permute-done((bf16[48,2048]{1,0:T(8,128)(2,1)}, bf16[48,2048]{1,0:T(8,128)(2,1)S(1)}, u32[]{:S(2)}, u32[]{:S(2)}) %collective-permute-start) | collective-permute-done | bytes 196640 | tf_op jit(solution)/shard_map/while/body/eval_jaxpr/ppermute | solution.py:11
  501.7 7.4 %collective-permute-done = bf16[48,2048]{1,0:T(8,128)(2,1)S(1)} collective-permute-done((bf16[48,2048]{1,0:T(8,128)(2,1)}, bf16[48,2048]{1,0:T(8,128)(2,1)S(1)}, u32[]{:S(2)}, u32[]{:S(2)}) %collective-permute-start) | collective-permute-done | bytes 196640 | tf_op jit(solution)/shard_map/while/body/eval_jaxpr/ppermute | solution.py:11
  513.3 7.4 %collective-permute-done = bf16[48,2048]{1,0:T(8,128)(2,1)S(1)} collective-permute-done((bf16[48,2048]{1,0:T(8,128)(2,1)}, bf16[48,2048]{1,0:T(8,128)(2,1)S(1)}, u32[]{:S(2)}, u32[]{:S(2)}) %collective-permute-start) | collective-permute-done | bytes 196640 | tf_op jit(solution)/shard_map/while/body/eval_jaxpr/ppermute | solution.py:11
  (107 shorter events, 135.0 us)
Async XLA Ops:
  0.0 124.1 %copy-start = (f32[64,64]{1,0:T(8,128)S(1)}, f32[64,64]{1,0:T(8,128)}, u32[]{:S(2)}) copy-start(f32[64,64]{1,0:T(8,128)} %param.11) | copy-start | bytes 49156
  1.5 21.4 %all-to-all-start.1 = ((bf16[16,3,2048]{2,1,0:T(4,128)(2,1)}), bf16[16,3,2048]{2,1,0:T(4,128)(2,1)S(1)}, u32[]{:S(2)}, u32[]{:S(2)}) async-start(bf16[16,3,2048]{2,1,0:T(4,128)(2,1)} %stack.2), calls=%async_computation.1 | async-start | bytes 524288 | tf_op jit(solution)/shard_map/all_to_all | solution.py:49
  22.9 93.6 %all-to-all-start = ((bf16[32,24,2048]{2,1,0:T(8,128)(2,1)}), bf16[32,24,2048]{2,1,0:T(8,128)(2,1)S(1)}, u32[]{:S(2)}, u32[]{:S(2)}) async-start(bf16[32,24,2048]{2,1,0:T(8,128)(2,1)} %bitcast.2), calls=%async_computation | async-start | bytes 6291456 | tf_op jit(solution)/shard_map/all_to_all | solution.py:58
  124.1 9.0 %copy-start.2 = (f32[32,32]{1,0:T(8,128)S(1)}, f32[32,32]{1,0:T(8,128)}, u32[]{:S(2)}) copy-start(f32[32,32]{1,0:T(8,128)} %param.10) | copy-start | bytes 12292
  160.0 1.4 copy-start.1
  161.4 9.3 %collective-permute-start = (bf16[48,2048]{1,0:T(8,128)(2,1)}, bf16[48,2048]{1,0:T(8,128)(2,1)S(1)}, u32[]{:S(2)}, u32[]{:S(2)}) collective-permute-start(bf16[48,2048]{1,0:T(8,128)(2,1)} %get-tuple-element.200), channel_id=1, source_target_pairs={{496,0},{0,16},{16,32},{32,48},{48,64},{64,80},{80,96},{96,112},{1... | collective-permute-start | bytes 589832 | tf_op jit(solution)/shard_map/while/body/eval_jaxpr/ppermute | solution.py:11
  173.1 9.3 %collective-permute-start = (bf16[48,2048]{1,0:T(8,128)(2,1)}, bf16[48,2048]{1,0:T(8,128)(2,1)S(1)}, u32[]{:S(2)}, u32[]{:S(2)}) collective-permute-start(bf16[48,2048]{1,0:T(8,128)(2,1)} %get-tuple-element.200), channel_id=1, source_target_pairs={{496,0},{0,16},{16,32},{32,48},{48,64},{64,80},{80,96},{96,112},{1... | collective-permute-start | bytes 589832 | tf_op jit(solution)/shard_map/while/body/eval_jaxpr/ppermute | solution.py:11
  184.7 9.3 %collective-permute-start = (bf16[48,2048]{1,0:T(8,128)(2,1)}, bf16[48,2048]{1,0:T(8,128)(2,1)S(1)}, u32[]{:S(2)}, u32[]{:S(2)}) collective-permute-start(bf16[48,2048]{1,0:T(8,128)(2,1)} %get-tuple-element.200), channel_id=1, source_target_pairs={{496,0},{0,16},{16,32},{32,48},{48,64},{64,80},{80,96},{96,112},{1... | collective-permute-start | bytes 589832 | tf_op jit(solution)/shard_map/while/body/eval_jaxpr/ppermute | solution.py:11
  196.4 9.3 %collective-permute-start = (bf16[48,2048]{1,0:T(8,128)(2,1)}, bf16[48,2048]{1,0:T(8,128)(2,1)S(1)}, u32[]{:S(2)}, u32[]{:S(2)}) collective-permute-start(bf16[48,2048]{1,0:T(8,128)(2,1)} %get-tuple-element.200), channel_id=1, source_target_pairs={{496,0},{0,16},{16,32},{32,48},{48,64},{64,80},{80,96},{96,112},{1... | collective-permute-start | bytes 589832 | tf_op jit(solution)/shard_map/while/body/eval_jaxpr/ppermute | solution.py:11
  208.1 9.3 %collective-permute-start = (bf16[48,2048]{1,0:T(8,128)(2,1)}, bf16[48,2048]{1,0:T(8,128)(2,1)S(1)}, u32[]{:S(2)}, u32[]{:S(2)}) collective-permute-start(bf16[48,2048]{1,0:T(8,128)(2,1)} %get-tuple-element.200), channel_id=1, source_target_pairs={{496,0},{0,16},{16,32},{32,48},{48,64},{64,80},{80,96},{96,112},{1... | collective-permute-start | bytes 589832 | tf_op jit(solution)/shard_map/while/body/eval_jaxpr/ppermute | solution.py:11
  219.7 9.3 %collective-permute-start = (bf16[48,2048]{1,0:T(8,128)(2,1)}, bf16[48,2048]{1,0:T(8,128)(2,1)S(1)}, u32[]{:S(2)}, u32[]{:S(2)}) collective-permute-start(bf16[48,2048]{1,0:T(8,128)(2,1)} %get-tuple-element.200), channel_id=1, source_target_pairs={{496,0},{0,16},{16,32},{32,48},{48,64},{64,80},{80,96},{96,112},{1... | collective-permute-start | bytes 589832 | tf_op jit(solution)/shard_map/while/body/eval_jaxpr/ppermute | solution.py:11
  231.4 9.3 %collective-permute-start = (bf16[48,2048]{1,0:T(8,128)(2,1)}, bf16[48,2048]{1,0:T(8,128)(2,1)S(1)}, u32[]{:S(2)}, u32[]{:S(2)}) collective-permute-start(bf16[48,2048]{1,0:T(8,128)(2,1)} %get-tuple-element.200), channel_id=1, source_target_pairs={{496,0},{0,16},{16,32},{32,48},{48,64},{64,80},{80,96},{96,112},{1... | collective-permute-start | bytes 589832 | tf_op jit(solution)/shard_map/while/body/eval_jaxpr/ppermute | solution.py:11
  243.1 9.3 %collective-permute-start = (bf16[48,2048]{1,0:T(8,128)(2,1)}, bf16[48,2048]{1,0:T(8,128)(2,1)S(1)}, u32[]{:S(2)}, u32[]{:S(2)}) collective-permute-start(bf16[48,2048]{1,0:T(8,128)(2,1)} %get-tuple-element.200), channel_id=1, source_target_pairs={{496,0},{0,16},{16,32},{32,48},{48,64},{64,80},{80,96},{96,112},{1... | collective-permute-start | bytes 589832 | tf_op jit(solution)/shard_map/while/body/eval_jaxpr/ppermute | solution.py:11
  254.7 9.3 %collective-permute-start = (bf16[48,2048]{1,0:T(8,128)(2,1)}, bf16[48,2048]{1,0:T(8,128)(2,1)S(1)}, u32[]{:S(2)}, u32[]{:S(2)}) collective-permute-start(bf16[48,2048]{1,0:T(8,128)(2,1)} %get-tuple-element.200), channel_id=1, source_target_pairs={{496,0},{0,16},{16,32},{32,48},{48,64},{64,80},{80,96},{96,112},{1... | collective-permute-start | bytes 589832 | tf_op jit(solution)/shard_map/while/body/eval_jaxpr/ppermute | solution.py:11
  266.4 9.3 %collective-permute-start = (bf16[48,2048]{1,0:T(8,128)(2,1)}, bf16[48,2048]{1,0:T(8,128)(2,1)S(1)}, u32[]{:S(2)}, u32[]{:S(2)}) collective-permute-start(bf16[48,2048]{1,0:T(8,128)(2,1)} %get-tuple-element.200), channel_id=1, source_target_pairs={{496,0},{0,16},{16,32},{32,48},{48,64},{64,80},{80,96},{96,112},{1... | collective-permute-start | bytes 589832 | tf_op jit(solution)/shard_map/while/body/eval_jaxpr/ppermute | solution.py:11
  278.1 9.3 %collective-permute-start = (bf16[48,2048]{1,0:T(8,128)(2,1)}, bf16[48,2048]{1,0:T(8,128)(2,1)S(1)}, u32[]{:S(2)}, u32[]{:S(2)}) collective-permute-start(bf16[48,2048]{1,0:T(8,128)(2,1)} %get-tuple-element.200), channel_id=1, source_target_pairs={{496,0},{0,16},{16,32},{32,48},{48,64},{64,80},{80,96},{96,112},{1... | collective-permute-start | bytes 589832 | tf_op jit(solution)/shard_map/while/body/eval_jaxpr/ppermute | solution.py:11
  289.7 9.3 %collective-permute-start = (bf16[48,2048]{1,0:T(8,128)(2,1)}, bf16[48,2048]{1,0:T(8,128)(2,1)S(1)}, u32[]{:S(2)}, u32[]{:S(2)}) collective-permute-start(bf16[48,2048]{1,0:T(8,128)(2,1)} %get-tuple-element.200), channel_id=1, source_target_pairs={{496,0},{0,16},{16,32},{32,48},{48,64},{64,80},{80,96},{96,112},{1... | collective-permute-start | bytes 589832 | tf_op jit(solution)/shard_map/while/body/eval_jaxpr/ppermute | solution.py:11
  301.4 9.3 %collective-permute-start = (bf16[48,2048]{1,0:T(8,128)(2,1)}, bf16[48,2048]{1,0:T(8,128)(2,1)S(1)}, u32[]{:S(2)}, u32[]{:S(2)}) collective-permute-start(bf16[48,2048]{1,0:T(8,128)(2,1)} %get-tuple-element.200), channel_id=1, source_target_pairs={{496,0},{0,16},{16,32},{32,48},{48,64},{64,80},{80,96},{96,112},{1... | collective-permute-start | bytes 589832 | tf_op jit(solution)/shard_map/while/body/eval_jaxpr/ppermute | solution.py:11
  313.1 9.3 %collective-permute-start = (bf16[48,2048]{1,0:T(8,128)(2,1)}, bf16[48,2048]{1,0:T(8,128)(2,1)S(1)}, u32[]{:S(2)}, u32[]{:S(2)}) collective-permute-start(bf16[48,2048]{1,0:T(8,128)(2,1)} %get-tuple-element.200), channel_id=1, source_target_pairs={{496,0},{0,16},{16,32},{32,48},{48,64},{64,80},{80,96},{96,112},{1... | collective-permute-start | bytes 589832 | tf_op jit(solution)/shard_map/while/body/eval_jaxpr/ppermute | solution.py:11
  324.7 9.3 %collective-permute-start = (bf16[48,2048]{1,0:T(8,128)(2,1)}, bf16[48,2048]{1,0:T(8,128)(2,1)S(1)}, u32[]{:S(2)}, u32[]{:S(2)}) collective-permute-start(bf16[48,2048]{1,0:T(8,128)(2,1)} %get-tuple-element.200), channel_id=1, source_target_pairs={{496,0},{0,16},{16,32},{32,48},{48,64},{64,80},{80,96},{96,112},{1... | collective-permute-start | bytes 589832 | tf_op jit(solution)/shard_map/while/body/eval_jaxpr/ppermute | solution.py:11
  336.4 9.3 %collective-permute-start = (bf16[48,2048]{1,0:T(8,128)(2,1)}, bf16[48,2048]{1,0:T(8,128)(2,1)S(1)}, u32[]{:S(2)}, u32[]{:S(2)}) collective-permute-start(bf16[48,2048]{1,0:T(8,128)(2,1)} %get-tuple-element.200), channel_id=1, source_target_pairs={{496,0},{0,16},{16,32},{32,48},{48,64},{64,80},{80,96},{96,112},{1... | collective-permute-start | bytes 589832 | tf_op jit(solution)/shard_map/while/body/eval_jaxpr/ppermute | solution.py:11
  348.1 9.3 %collective-permute-start = (bf16[48,2048]{1,0:T(8,128)(2,1)}, bf16[48,2048]{1,0:T(8,128)(2,1)S(1)}, u32[]{:S(2)}, u32[]{:S(2)}) collective-permute-start(bf16[48,2048]{1,0:T(8,128)(2,1)} %get-tuple-element.200), channel_id=1, source_target_pairs={{496,0},{0,16},{16,32},{32,48},{48,64},{64,80},{80,96},{96,112},{1... | collective-permute-start | bytes 589832 | tf_op jit(solution)/shard_map/while/body/eval_jaxpr/ppermute | solution.py:11
  359.7 9.3 %collective-permute-start = (bf16[48,2048]{1,0:T(8,128)(2,1)}, bf16[48,2048]{1,0:T(8,128)(2,1)S(1)}, u32[]{:S(2)}, u32[]{:S(2)}) collective-permute-start(bf16[48,2048]{1,0:T(8,128)(2,1)} %get-tuple-element.200), channel_id=1, source_target_pairs={{496,0},{0,16},{16,32},{32,48},{48,64},{64,80},{80,96},{96,112},{1... | collective-permute-start | bytes 589832 | tf_op jit(solution)/shard_map/while/body/eval_jaxpr/ppermute | solution.py:11
  371.4 9.3 %collective-permute-start = (bf16[48,2048]{1,0:T(8,128)(2,1)}, bf16[48,2048]{1,0:T(8,128)(2,1)S(1)}, u32[]{:S(2)}, u32[]{:S(2)}) collective-permute-start(bf16[48,2048]{1,0:T(8,128)(2,1)} %get-tuple-element.200), channel_id=1, source_target_pairs={{496,0},{0,16},{16,32},{32,48},{48,64},{64,80},{80,96},{96,112},{1... | collective-permute-start | bytes 589832 | tf_op jit(solution)/shard_map/while/body/eval_jaxpr/ppermute | solution.py:11
  383.1 9.3 %collective-permute-start = (bf16[48,2048]{1,0:T(8,128)(2,1)}, bf16[48,2048]{1,0:T(8,128)(2,1)S(1)}, u32[]{:S(2)}, u32[]{:S(2)}) collective-permute-start(bf16[48,2048]{1,0:T(8,128)(2,1)} %get-tuple-element.200), channel_id=1, source_target_pairs={{496,0},{0,16},{16,32},{32,48},{48,64},{64,80},{80,96},{96,112},{1... | collective-permute-start | bytes 589832 | tf_op jit(solution)/shard_map/while/body/eval_jaxpr/ppermute | solution.py:11
  394.7 9.3 %collective-permute-start = (bf16[48,2048]{1,0:T(8,128)(2,1)}, bf16[48,2048]{1,0:T(8,128)(2,1)S(1)}, u32[]{:S(2)}, u32[]{:S(2)}) collective-permute-start(bf16[48,2048]{1,0:T(8,128)(2,1)} %get-tuple-element.200), channel_id=1, source_target_pairs={{496,0},{0,16},{16,32},{32,48},{48,64},{64,80},{80,96},{96,112},{1... | collective-permute-start | bytes 589832 | tf_op jit(solution)/shard_map/while/body/eval_jaxpr/ppermute | solution.py:11
  406.4 9.3 %collective-permute-start = (bf16[48,2048]{1,0:T(8,128)(2,1)}, bf16[48,2048]{1,0:T(8,128)(2,1)S(1)}, u32[]{:S(2)}, u32[]{:S(2)}) collective-permute-start(bf16[48,2048]{1,0:T(8,128)(2,1)} %get-tuple-element.200), channel_id=1, source_target_pairs={{496,0},{0,16},{16,32},{32,48},{48,64},{64,80},{80,96},{96,112},{1... | collective-permute-start | bytes 589832 | tf_op jit(solution)/shard_map/while/body/eval_jaxpr/ppermute | solution.py:11
  418.1 9.3 %collective-permute-start = (bf16[48,2048]{1,0:T(8,128)(2,1)}, bf16[48,2048]{1,0:T(8,128)(2,1)S(1)}, u32[]{:S(2)}, u32[]{:S(2)}) collective-permute-start(bf16[48,2048]{1,0:T(8,128)(2,1)} %get-tuple-element.200), channel_id=1, source_target_pairs={{496,0},{0,16},{16,32},{32,48},{48,64},{64,80},{80,96},{96,112},{1... | collective-permute-start | bytes 589832 | tf_op jit(solution)/shard_map/while/body/eval_jaxpr/ppermute | solution.py:11
  429.7 9.3 %collective-permute-start = (bf16[48,2048]{1,0:T(8,128)(2,1)}, bf16[48,2048]{1,0:T(8,128)(2,1)S(1)}, u32[]{:S(2)}, u32[]{:S(2)}) collective-permute-start(bf16[48,2048]{1,0:T(8,128)(2,1)} %get-tuple-element.200), channel_id=1, source_target_pairs={{496,0},{0,16},{16,32},{32,48},{48,64},{64,80},{80,96},{96,112},{1... | collective-permute-start | bytes 589832 | tf_op jit(solution)/shard_map/while/body/eval_jaxpr/ppermute | solution.py:11
  441.4 9.3 %collective-permute-start = (bf16[48,2048]{1,0:T(8,128)(2,1)}, bf16[48,2048]{1,0:T(8,128)(2,1)S(1)}, u32[]{:S(2)}, u32[]{:S(2)}) collective-permute-start(bf16[48,2048]{1,0:T(8,128)(2,1)} %get-tuple-element.200), channel_id=1, source_target_pairs={{496,0},{0,16},{16,32},{32,48},{48,64},{64,80},{80,96},{96,112},{1... | collective-permute-start | bytes 589832 | tf_op jit(solution)/shard_map/while/body/eval_jaxpr/ppermute | solution.py:11
  453.1 9.3 %collective-permute-start = (bf16[48,2048]{1,0:T(8,128)(2,1)}, bf16[48,2048]{1,0:T(8,128)(2,1)S(1)}, u32[]{:S(2)}, u32[]{:S(2)}) collective-permute-start(bf16[48,2048]{1,0:T(8,128)(2,1)} %get-tuple-element.200), channel_id=1, source_target_pairs={{496,0},{0,16},{16,32},{32,48},{48,64},{64,80},{80,96},{96,112},{1... | collective-permute-start | bytes 589832 | tf_op jit(solution)/shard_map/while/body/eval_jaxpr/ppermute | solution.py:11
  464.7 9.3 %collective-permute-start = (bf16[48,2048]{1,0:T(8,128)(2,1)}, bf16[48,2048]{1,0:T(8,128)(2,1)S(1)}, u32[]{:S(2)}, u32[]{:S(2)}) collective-permute-start(bf16[48,2048]{1,0:T(8,128)(2,1)} %get-tuple-element.200), channel_id=1, source_target_pairs={{496,0},{0,16},{16,32},{32,48},{48,64},{64,80},{80,96},{96,112},{1... | collective-permute-start | bytes 589832 | tf_op jit(solution)/shard_map/while/body/eval_jaxpr/ppermute | solution.py:11
  476.4 9.3 %collective-permute-start = (bf16[48,2048]{1,0:T(8,128)(2,1)}, bf16[48,2048]{1,0:T(8,128)(2,1)S(1)}, u32[]{:S(2)}, u32[]{:S(2)}) collective-permute-start(bf16[48,2048]{1,0:T(8,128)(2,1)} %get-tuple-element.200), channel_id=1, source_target_pairs={{496,0},{0,16},{16,32},{32,48},{48,64},{64,80},{80,96},{96,112},{1... | collective-permute-start | bytes 589832 | tf_op jit(solution)/shard_map/while/body/eval_jaxpr/ppermute | solution.py:11
  488.1 9.3 %collective-permute-start = (bf16[48,2048]{1,0:T(8,128)(2,1)}, bf16[48,2048]{1,0:T(8,128)(2,1)S(1)}, u32[]{:S(2)}, u32[]{:S(2)}) collective-permute-start(bf16[48,2048]{1,0:T(8,128)(2,1)} %get-tuple-element.200), channel_id=1, source_target_pairs={{496,0},{0,16},{16,32},{32,48},{48,64},{64,80},{80,96},{96,112},{1... | collective-permute-start | bytes 589832 | tf_op jit(solution)/shard_map/while/body/eval_jaxpr/ppermute | solution.py:11
  499.7 9.3 %collective-permute-start = (bf16[48,2048]{1,0:T(8,128)(2,1)}, bf16[48,2048]{1,0:T(8,128)(2,1)S(1)}, u32[]{:S(2)}, u32[]{:S(2)}) collective-permute-start(bf16[48,2048]{1,0:T(8,128)(2,1)} %get-tuple-element.200), channel_id=1, source_target_pairs={{496,0},{0,16},{16,32},{32,48},{48,64},{64,80},{80,96},{96,112},{1... | collective-permute-start | bytes 589832 | tf_op jit(solution)/shard_map/while/body/eval_jaxpr/ppermute | solution.py:11
  511.4 9.3 %collective-permute-start = (bf16[48,2048]{1,0:T(8,128)(2,1)}, bf16[48,2048]{1,0:T(8,128)(2,1)S(1)}, u32[]{:S(2)}, u32[]{:S(2)}) collective-permute-start(bf16[48,2048]{1,0:T(8,128)(2,1)} %get-tuple-element.200), channel_id=1, source_target_pairs={{496,0},{0,16},{16,32},{32,48},{48,64},{64,80},{80,96},{96,112},{1... | collective-permute-start | bytes 589832 | tf_op jit(solution)/shard_map/while/body/eval_jaxpr/ppermute | solution.py:11
